TPU v7x, 256 devices: a whole 4x4x8 slice. The times are simulated.
256 devices in a mesh: occ: 8 (over x_lo, y), vir: 32 (over x_hi, z, core).
Axes of the slice: x: 4 (x_hi: 2, x_lo: 2; x = x_hi * 2 + x_lo), y: 4, z: 8, core: 2. Of those that a mesh axis runs over, the one named last changes fastest.
Arguments:
- amplitudes: bfloat16 [64, 64, 131072], P('occ', None, 'vir'), may hold values from -6 to 6
- integrals: bfloat16 [131072, 1024], P('vir'), may hold values from -0.03125 to 0.03125
- occ_irrep: int32 [64], replicated, may hold values from 0 to 7
- vir_irrep: int32 [32], replicated, may hold values from 0 to 7
Outputs:
- ladder: float32 [32, 64, 2048], P('vir', 'occ')
Inputs may be any that keep to these rules, and one draw needn't show every extreme that they name: `occ_irrep`: labels of the eight irreducible representations of D2h, multiplied by bitwise xor. `vir_irrep`: labels of the eight irreducible representations of D2h, multiplied by bitwise xor.
All inputs are finite; a program needn't handle non-finite values.
Results may differ from a plain program's by a relative error of at most 0.0003.
Values sent between devices are 32-bit elements; how exact they have to be, the bound alone decides.
A program may use at most 64 MiB of HBM per device.

v0:
```python
import jax
import jax.numpy as jnp
from jax import lax
from jax.sharding import PartitionSpec as P


def shards(amplitudes, integrals, occ_irrep, vir_irrep):
    occ_rows = amplitudes.shape[0]
    width = occ_irrep.shape[0]
    panel = vir_irrep.shape[0]
    vir_rows = panel // lax.axis_size("vir")
    flat = amplitudes.reshape(occ_rows * width, amplitudes.shape[2])
    product = jnp.dot(flat, integrals, preferred_element_type=jnp.float32)
    product = product.reshape(occ_rows, width, lax.axis_size("vir") * vir_rows, panel)
    summed = lax.psum_scatter(
        jnp.transpose(product, (2, 0, 1, 3)).reshape(
            lax.axis_size("vir") * vir_rows, occ_rows, width * panel
        ),
        "vir",
        scatter_dimension=0,
        tiled=True,
    )
    summed = summed.reshape(vir_rows, occ_rows, width, panel)
    moved = lax.all_to_all(summed, "vir", split_axis=3, concat_axis=0, tiled=True)
    pairab = summed - jnp.transpose(moved, (3, 1, 2, 0))
    partner = lax.all_to_all(pairab, "occ", split_axis=2, concat_axis=1, tiled=True)
    pairij = pairab - jnp.transpose(partner, (0, 2, 1, 3))
    occ_start = lax.axis_index("occ") * occ_rows
    vir_start = lax.axis_index("vir") * vir_rows
    occ_local = lax.dynamic_slice_in_dim(occ_irrep, occ_start, occ_rows, 0)
    vir_local = lax.dynamic_slice_in_dim(vir_irrep, vir_start, vir_rows, 0)
    label = (
        vir_local[:, None, None, None]
        ^ occ_local[None, :, None, None]
        ^ occ_irrep[None, None, :, None]
        ^ vir_irrep[None, None, None, :]
    )
    masked = jnp.where(label == 0, pairij, jnp.zeros_like(pairij))
    return masked.reshape(vir_rows, occ_rows, width * panel)


def solution(mesh):
    placed = (P("occ", None, "vir"), P("vir", None), P(), P())
    return jax.shard_map(
        shards, mesh=mesh, in_specs=placed, out_specs=P("vir", "occ", None), check_vma=False
    )
```

profile of v0, /device:TPU:1, one launch (start us, length us, event | category | flops | bytes accessed | tf_op | source)
XLA Modules:
  0.0 208.8 jit_solution(3835859853237761105)
XLA Ops:
  6.5 0.0 reduce-scatter.2.cloned.1.call-start
  6.5 11.8 %copy.10 = bf16[4096,1024]{0,1:T(8,128)(2,1)} copy(bf16[4096,1024]{1,0:T(8,128)(2,1)} %param.5) | data formatting | bytes 16777216 | tf_op args[1]
  18.3 13.9 %fusion.2 = f32[32,8,64,32]{2,3,0,1:T(8,128)} fusion(bf16[32,32,4096,1]{2,1,0,3:T(8,128)(2,1)} %bitcast.42, bf16[8,64,4096]{2,1,0:T(8,128)(2,1)} %param.4), kind=kOutput, calls=%fused_computation.2 | convolution fusion | flops 4294967296 | bytes 14680064 | tf_op jit(solution)/shard_map/dot_general | solution.py:13
  32.2 6.9 %copy.11 = f32[32,8,64,32]{3,2,1,0:T(8,128)} copy(f32[32,8,64,32]{2,3,0,1:T(8,128)} %fusion.2) | data formatting | bytes 4194304 | tf_op jit(solution)/shard_map/transpose | solution.py:16
  39.1 0.0 copy-start.1
  39.1 0.0 copy-start
  39.1 7.5 %reshape.65 = f32[32,8,2048]{2,1,0:T(8,128)} reshape(f32[32,8,64,32]{3,2,1,0:T(8,128)} %copy.11) | data formatting | bytes 4194304 | tf_op jit(solution)/shard_map/reshape | solution.py:16
  46.7 0.0 reduce-scatter.2.cloned.1.call-update
  46.7 118.2 %reduce-scatter.2.cloned.1.call-done = f32[1,8,2048]{2,1,0:T(8,128)} async-done(((f32[32,8,2048]{2,1,0:T(8,128)}), f32[1,8,2048]{2,1,0:T(8,128)}) %reduce-scatter.2.cloned.1.call-update) | async-done | bytes 65552 | tf_op jit(solution)/shard_map/reduce_scatter | solution.py:15
  164.8 1.0 reshape.66
  165.8 0.1 copy.12
  165.9 0.8 reshape.70
  166.7 11.5 %all-to-all-start = ((f32[32,1,512]{2,1,0:T(1,128)}), f32[32,1,512]{2,1,0:T(1,128)S(1)}, u32[]{:S(2)}, u32[]{:S(2)}) async-start(f32[32,1,512]{2,1,0:T(1,128)} %reshape.70), calls=%async_computation.1 | async-start | bytes 131072 | tf_op jit(solution)/shard_map/all_to_all | solution.py:24
  178.2 0.0 copy-done.1
  178.2 0.6 dynamic_slice.6
  178.8 0.0 copy-done
  178.8 0.6 dynamic-slice_xor_fusion
  179.4 8.3 %all-to-all-done = f32[32,1,512]{2,1,0:T(1,128)S(1)} async-done(((f32[32,1,512]{2,1,0:T(1,128)}), f32[32,1,512]{2,1,0:T(1,128)S(1)}, u32[]{:S(2)}, u32[]{:S(2)}) %all-to-all-start) | async-done | bytes 65568 | tf_op jit(solution)/shard_map/all_to_all | solution.py:24
  187.7 0.5 broadcast.55
  188.2 0.7 reduce
  189.0 0.1 reshape.71
  189.1 0.1 copy.13
  189.2 0.2 copy.19
  189.4 0.8 reshape.72
  190.2 4.8 %all-to-all-start.1 = ((f32[8,1,2048]{2,1,0:T(1,128)}), f32[8,1,2048]{2,1,0:T(1,128)S(1)}, u32[]{:S(2)}, u32[]{:S(2)}) async-start(f32[8,1,2048]{2,1,0:T(1,128)} %reshape.72), calls=%async_computation.2 | async-start | bytes 131072 | tf_op jit(solution)/shard_map/all_to_all | solution.py:26
  195.0 0.1 broadcast_xor_fusion
  195.1 5.1 %all-to-all-done.1 = f32[8,1,2048]{2,1,0:T(1,128)S(1)} async-done(((f32[8,1,2048]{2,1,0:T(1,128)}), f32[8,1,2048]{2,1,0:T(1,128)S(1)}, u32[]{:S(2)}, u32[]{:S(2)}) %all-to-all-start.1) | async-done | bytes 65568 | tf_op jit(solution)/shard_map/all_to_all | solution.py:26
  200.2 0.7 reduce.1
  201.0 0.1 reshape.73
  201.1 0.1 fusion.5
  201.2 0.8 reshape.67
  (1 shorter events, 0.0 us)
Async XLA Ops:
  6.5 158.3 %reduce-scatter.2.cloned.1.call-start = ((), (), s32[]{:S(2)}) async-start(), calls=%async_computation.3 | async-start | bytes 2162688 | tf_op jit(solution)/shard_map/reduce_scatter | solution.py:15
  39.1 139.0 %copy-start.1 = (s32[32]{0:T(128)S(1)}, s32[32]{0:T(128)}, u32[]{:S(2)}) copy-start(s32[32]{0:T(128)} %param.7) | copy-start | bytes 388
  39.1 139.6 %copy-start = (s32[64]{0:T(128)S(1)}, s32[64]{0:T(128)}, u32[]{:S(2)}) copy-start(s32[64]{0:T(128)} %param.6) | copy-start | bytes 772
  166.7 21.0 %all-to-all-start = ((f32[32,1,512]{2,1,0:T(1,128)}), f32[32,1,512]{2,1,0:T(1,128)S(1)}, u32[]{:S(2)}, u32[]{:S(2)}) async-start(f32[32,1,512]{2,1,0:T(1,128)} %reshape.70), calls=%async_computation.1 | async-start | bytes 131072 | tf_op jit(solution)/shard_map/all_to_all | solution.py:24
  190.2 10.0 %all-to-all-start.1 = ((f32[8,1,2048]{2,1,0:T(1,128)}), f32[8,1,2048]{2,1,0:T(1,128)S(1)}, u32[]{:S(2)}, u32[]{:S(2)}) async-start(f32[8,1,2048]{2,1,0:T(1,128)} %reshape.72), calls=%async_computation.2 | async-start | bytes 131072 | tf_op jit(solution)/shard_map/all_to_all | solution.py:26
Sparse Core Ops, SparseCore 0:
  46.8 117.9 reduce-scatter.1
where the time goes:
time: 210 us; the launch traced here: 209 us
  waiting for transfers between devices  132 us (63%)
  local copies, waits for them, and re-layouts  31.2 us (15%)
  starting transfers between devices  16.3 us (8%)
  matrix products  13.9 us (7%)
  between operations  13.5 us (6%)
  other arithmetic  2.3 us (1%)
    reduce_scatter x1, waiting for transfers between devices, shards(): lax.psum_scatter(jnp.transpose(product, (2, 0, 1, 3)).reshape(lax.axis_si...  118 us
    dot_general x1, matrix products, shards(): product = jnp.dot(flat, integrals, preferred_element_type=jnp.float32)  13.9 us
    unnamed x9, local copies, waits for them, and re-layouts  13.6 us
    all_to_all x1, starting transfers between devices, shards(): lax.all_to_all(summed, 'vir', split_axis=3, concat_axis=0, tiled=True)  11.5 us
    all_to_all x1, waiting for transfers between devices, shards(): lax.all_to_all(summed, 'vir', split_axis=3, concat_axis=0, tiled=True)  8.35 us
    reshape x1, local copies, waits for them, and re-layouts, shards(): jnp.transpose(product, (2, 0, 1, 3))  7.52 us
    transpose x1, local copies, waits for them, and re-layouts, shards(): jnp.transpose(product, (2, 0, 1, 3))  6.94 us
    all_to_all x1, waiting for transfers between devices, shards(): lax.all_to_all(pairab, 'occ', split_axis=2, concat_axis=1, tiled=True)  5.13 us
  transfers between devices with their start and end apart: 3, of which 3 were waited for; matrix products, arithmetic and copies ran while one was open for 1% of the time, Pallas kernels for 0%

commit v1 on v0

v1 whole, which is shorter than its diff:
```python
import functools

import jax
import jax.numpy as jnp
from jax import lax
from jax.experimental import pallas as pl
from jax.experimental.pallas import tpu as pltpu
from jax.sharding import PartitionSpec as P

MESH = pl.DeviceIdType.MESH
F32, BF16, I32 = jnp.float32, jnp.bfloat16, jnp.int32
CHIPS, Z, CORES, OCC = 16, 8, 2, 8
NB = 32
KC, NK = 512, 8


def iota(shape, dim):
    return lax.broadcasted_iota(I32, shape, dim)


def kernel(
    amp, vint, occ_ref, vir_ref, out_ref,
    a_sib, a_own, v_buf, x_sib, x_own, x_got, hi, lo, sel, y_buf, y_got, u_buf, ut_buf,
    m_buf, t_buf, m_got, t_got, flags,
    sem_as, sem_ao, sem_v, s1_send, s1_recv, s2_send, s2_recv, s3_send, s3_recv, m_send, m_recv,
):
    occ = lax.axis_index("occ")
    vir = lax.axis_index("vir")
    chip = vir // CORES
    core = vir % CORES
    sibling = (occ, chip * CORES + 1 - core)

    def load_as(k):
        return pltpu.make_async_copy(
            amp.at[:, pl.ds(32 * (1 - core), 32), pl.ds(k * KC, KC)], a_sib.at[k], sem_as.at[k])

    def load_v(k):
        return pltpu.make_async_copy(
            vint.at[pl.ds(k * KC, KC), :], v_buf.at[pl.ds(k * KC, KC), :], sem_v.at[k])

    load_ao = pltpu.make_async_copy(amp.at[:, pl.ds(32 * core, 32), :], a_own, sem_ao.at[0])
    for k in range(NK):
        load_as(k).start()
        load_v(k).start()
    load_ao.start()

    barrier = pltpu.get_barrier_semaphore()
    for d in range(1, CHIPS):
        to = (occ, ((chip + d) % CHIPS) * CORES + core)
        pl.semaphore_signal(barrier, inc=1, device_id=to, device_id_type=MESH)
    for d in range(OCC):
        for c in range(CORES):
            if (d, c) != (0, 0):
                to = ((occ + d) % OCC, chip * CORES + (core + c) % CORES)
                pl.semaphore_signal(barrier, inc=1, device_id=to, device_id_type=MESH)

    xh, zh = chip // Z, (chip % Z) // 4
    blocks = []
    for step, (dx, dz) in enumerate(((1, 1), (0, 1), (1, 0), (0, 0))):
        blocks.append(((xh + dx) % 2) * 2 + (zh + dz) % 2)
    col, row = iota((NB, 1024), 1), iota((NB, 1024), 0)
    direct, swapped = col - row, col - NB * row
    for step in range(4):
        def build(al, carry, step=step):
            a = blocks[step] * 8 + al
            plus = jnp.where(direct == NB * a, 1.0, 0.0)
            minus = jnp.where(swapped == a, 1.0, 0.0)
            sel[step, pl.ds(pl.multiple_of(al * NB, NB), NB), :] = (plus - minus).astype(BF16)
            return carry
        lax.fori_loop(0, 8, build, 0)

    def first(k, carry):
        load_as(k).wait()
        load_v(k).wait()
        lhs = a_sib[k].reshape(256, KC)
        rhs = v_buf[pl.ds(pl.multiple_of(k * KC, KC), KC), :]
        part = jnp.dot(lhs, rhs, preferred_element_type=F32)

        @pl.when(k == 0)
        def _():
            x_sib[...] = part

        @pl.when(k > 0)
        def _():
            x_sib[...] += part
        return carry

    lax.fori_loop(0, NK, first, 0)
    pl.semaphore_wait(barrier, CHIPS - 1 + OCC * CORES - 1)
    s1 = pltpu.make_async_remote_copy(
        src_ref=x_sib, dst_ref=x_got, send_sem=s1_send, recv_sem=s1_recv,
        device_id=sibling, device_id_type=MESH)
    s1.start()

    load_ao.wait()
    for n in range(4):
        cols = pl.ds(n * 256, 256)
        x_own[:, cols] = jnp.dot(
            a_own[...].reshape(256, NK * KC), v_buf[:, cols], preferred_element_type=F32)
    s1.wait_recv()
    for n in range(4):
        cols = pl.ds(n * 256, 256)
        x = x_own[:, cols] + x_got[:, cols]
        top = x.astype(BF16)
        hi[:, cols] = top
        lo[:, cols] = (x - top.astype(F32)).astype(BF16)

    nt = (((1,), (1,)), ((), ()))

    def s2_copy(step, g):
        target = blocks[step] * 4 + g
        slot = (chip - target + CHIPS) % CHIPS
        return target, pltpu.make_async_remote_copy(
            src_ref=y_buf.at[step, g], dst_ref=y_got.at[slot],
            send_sem=s2_send.at[step * 4 + g], recv_sem=s2_recv.at[slot],
            device_id=(occ, target * CORES + core), device_id_type=MESH)

    for step in range(4):
        y = lax.dot_general(sel[step], hi[...], nt, preferred_element_type=F32)
        y = y + lax.dot_general(sel[step], lo[...], nt, preferred_element_type=F32)
        y_buf[step] = y.reshape(4, 64, 256)
        for g in range(4):
            target, copy = s2_copy(step, g)
            if step < 3:
                copy.start()
            else:
                pl.when(target != chip)(copy.start)

    occ_row = occ_ref[...].reshape(1, 64)
    vir_row = vir_ref[...].reshape(1, NB)

    total = y_buf[3, chip % 4]
    for d in range(1, CHIPS):
        s2_in = pltpu.make_async_remote_copy(
            src_ref=y_buf.at[0, 0], dst_ref=y_got.at[d],
            send_sem=s2_send.at[0], recv_sem=s2_recv.at[d],
            device_id=sibling, device_id_type=MESH)
        s2_in.wait_recv()
        total = total + y_got[d]
    u_buf[0:64, :] = total
    u_buf[64:128, :] = jnp.zeros((64, 256), F32)
    ut_buf[...] = jnp.transpose(u_buf[...])

    lane = iota((8, 128), 1) // NB

    def place(pieces, a):
        got = None
        for n, piece in enumerate(pieces):
            shift = ((n - a) * NB) % 128
            moved = pltpu.roll(piece, shift, 1) if shift else piece
            got = moved if got is None else jnp.where(lane == n, moved, got)
        return got

    for jl in range(4):
        for half in range(2):
            lanes = pl.ds(half * 128, 128)
            rows = [ut_buf[pl.ds((4 * half + n) * 32 + jl * 8, 8), :] for n in range(4)]
            for a in range(2):
                t_buf[a, jl, :, lanes] = place(rows, a)

    def s3_copy(jl, a):
        to = 4 * core + jl
        return pltpu.make_async_remote_copy(
            src_ref=t_buf.at[a, jl], dst_ref=t_got.at[occ],
            send_sem=s3_send.at[a * 4 + jl], recv_sem=s3_recv.at[occ],
            device_id=(to, chip * CORES + a), device_id_type=MESH)

    def s3_local(jl, a):
        return pltpu.make_async_copy(t_buf.at[a, jl], t_got.at[occ], s3_send.at[a * 4 + jl])

    for jl in range(4):
        for a in range(2):
            here = jnp.logical_and(4 * core + jl == occ, core == a)
            pl.when(jnp.logical_not(here))(s3_copy(jl, a).start)
            pl.when(here)(s3_local(jl, a).start)

    for jl in range(4):
        for half in range(2):
            lanes = pl.ds(half * 128, 128)
            rows = [ut_buf[pl.ds(jl * 8 + half * 4 + n, 8, stride=32), :] for n in range(4)]
            for a in range(2):
                m_buf[a, jl, :, lanes] = place(rows, a)
    m_copy = pltpu.make_async_remote_copy(
        src_ref=m_buf.at[1 - core], dst_ref=m_got, send_sem=m_send, recv_sem=m_recv,
        device_id=sibling, device_id_type=MESH)
    m_copy.start()

    spread = (iota((64, 2048), 1) // NB == iota((64, 2048), 0)).astype(F32)
    occ_all = jnp.broadcast_to(occ_row.astype(F32), (8, 64))
    occ_j = jnp.dot(occ_all, spread, preferred_element_type=F32)
    spread = (iota((NB, 2048), 1) % NB == iota((NB, 2048), 0)).astype(F32)
    vir_all = jnp.broadcast_to(vir_row.astype(F32), (8, NB))
    vir_b = jnp.dot(vir_all, spread, preferred_element_type=F32)
    mine = iota((8, 64), 1) == occ * 8 + iota((8, 64), 0)
    occ_i = jnp.sum(jnp.where(mine, occ_all, 0.0), axis=1, keepdims=True)
    vir_a = jnp.sum(jnp.where(iota((8, NB), 1) == vir, vir_all, 0.0), axis=1, keepdims=True)
    left = occ_j.astype(I32) ^ vir_b.astype(I32)
    right = occ_i.astype(I32) ^ vir_a.astype(I32)
    keep = (left ^ right) == 0
    for j in range(8):
        flags[j * 8:j * 8 + 8, :] = jnp.where(keep[:, j * 256:(j + 1) * 256], 1.0, 0.0)

    here = (occ // 4 == core)
    for d in range(OCC):
        incoming = pltpu.make_async_remote_copy(
            src_ref=t_buf.at[0, 0], dst_ref=t_got.at[d], send_sem=s3_send.at[0],
            recv_sem=s3_recv.at[d], device_id=sibling, device_id_type=MESH)
        local = jnp.logical_and(here, occ == d)
        pl.when(jnp.logical_not(local))(incoming.wait_recv)
    for jl in range(4):
        for a in range(2):
            own = jnp.logical_and(4 * core + jl == occ, core == a)
            pl.when(jnp.logical_not(own))(s3_copy(jl, a).wait_send)
            pl.when(own)(s3_local(jl, a).wait)
    m_copy.wait_recv()

    for jl in range(4):
        for part, src in ((core, m_buf.at[core, jl]), (1 - core, m_got.at[jl])):
            j = part * 4 + jl
            value = src[...] - t_got[j]
            flag = flags[pl.ds(pl.multiple_of(j * 8, 8), 8), :]
            out_ref[0, :, pl.ds(pl.multiple_of(j * 256, 256), 256)] = jnp.where(flag > 0.5, value, 0.0)

    m_copy.wait_send()
    s1.wait_send()
    for step in range(4):
        for g in range(4):
            target, copy = s2_copy(step, g)
            if step < 3:
                copy.wait_send()
            else:
                pl.when(target != chip)(copy.wait_send)


def shards(amplitudes, integrals, occ_irrep, vir_irrep):
    any_space = pl.BlockSpec(memory_space=pl.ANY)
    vmem = pl.BlockSpec(memory_space=pltpu.VMEM)
    dma = pltpu.SemaphoreType.DMA
    return pl.pallas_call(
        kernel,
        out_shape=jax.ShapeDtypeStruct((1, 8, 2048), F32),
        in_specs=[any_space, any_space, vmem, vmem],
        out_specs=vmem,
        scratch_shapes=[
            pltpu.VMEM((NK, 8, 32, KC), BF16),
            pltpu.VMEM((8, 32, NK * KC), BF16),
            pltpu.VMEM((NK * KC, 1024), BF16),
            pltpu.VMEM((256, 1024), F32),
            pltpu.VMEM((256, 1024), F32),
            pltpu.VMEM((256, 1024), F32),
            pltpu.VMEM((256, 1024), BF16),
            pltpu.VMEM((256, 1024), BF16),
            pltpu.VMEM((4, 256, 1024), BF16),
            pltpu.VMEM((4, 4, 64, 256), F32),
            pltpu.VMEM((CHIPS, 64, 256), F32),
            pltpu.VMEM((128, 256), F32),
            pltpu.VMEM((256, 128), F32),
            pltpu.VMEM((2, 4, 8, 256), F32),
            pltpu.VMEM((2, 4, 8, 256), F32),
            pltpu.VMEM((4, 8, 256), F32),
            pltpu.VMEM((8, 8, 256), F32),
            pltpu.VMEM((64, 256), F32),
            dma((NK,)), dma((1,)), dma((NK,)), dma, dma,
            dma((16,)), dma((16,)), dma((8,)), dma((8,)), dma, dma,
        ],
        compiler_params=pltpu.CompilerParams(
            collective_id=0, has_side_effects=True, vmem_limit_bytes=56 << 20),
        cost_estimate=pl.CostEstimate(
            flops=5_400_000_000, bytes_accessed=13_000_000, transcendentals=0),
        name="ladder",
    )(amplitudes, integrals, occ_irrep, vir_irrep)


def solution(mesh):
    placed = (P("occ", None, "vir"), P("vir", None), P(), P())
    return jax.shard_map(
        shards, mesh=mesh, in_specs=placed, out_specs=P("vir", "occ", None), check_vma=False
    )
```

time: 210 us -> 47.4 us (0.23)
  waiting for transfers between devices: 132 us -> 0 us
  Pallas kernels: 0 us -> 45.8 us
  local copies, waits for them, and re-layouts: 31.2 us -> 1.47 us
  starting transfers between devices: 16.3 us -> 0 us
  matrix products: 13.9 us -> 0 us
  between operations: 13.5 us -> 0.01 us
  other arithmetic: 2.3 us -> 0 us
    reduce_scatter x1 -> x0, waiting for transfers between devices: 118 us -> none  [shards(): lax.psum_scatter(jnp.transpose(product, (2, 0, 1, 3)).reshape(lax.axis_si...]
    pallas_call x0 -> x1, Pallas kernels: none -> 45.8 us  [shards(): pl.pallas_call(kernel, out_shape=jax.ShapeDtypeStruct((1, 8, 2048), F32),...]
    all_to_all x2 -> x0, starting transfers between devices: 16.3 us -> none  [the longest x1 11.5 us: shards(): lax.all_to_all(summed, 'vir', split_axis=3, concat_axis=0, tiled=True)]
    dot_general x1 -> x0, matrix products: 13.9 us -> none  [shards(): product = jnp.dot(flat, integrals, preferred_element_type=jnp.float32)]
    all_to_all x2 -> x0, waiting for transfers between devices: 13.5 us -> none  [the longest x1 8.35 us: shards(): lax.all_to_all(summed, 'vir', split_axis=3, concat_axis=0, tiled=True)]
    unnamed x9 -> x1, local copies, waits for them, and re-layouts: 13.6 us -> 1.47 us
    reshape x4 -> x0, local copies, waits for them, and re-layouts: 9.37 us -> none  [the longest x1 7.52 us: shards(): jnp.transpose(product, (2, 0, 1, 3))]
    transpose x1 -> x0, local copies, waits for them, and re-layouts: 6.94 us -> none  [shards(): jnp.transpose(product, (2, 0, 1, 3))]
  transfers between devices with their start and end apart: 3 -> 0, of which waited for: 3 -> 0; matrix products, arithmetic and copies ran while one was open for 1% -> 0% of each run, Pallas kernels for 0% -> 0%
where the time goes in v1:
time: 47.4 us; the launch traced here: 47.2 us
  Pallas kernels  45.8 us (97%)
  local copies, waits for them, and re-layouts  1.47 us (3%)
    pallas_call x1, Pallas kernels, shards(): pl.pallas_call(kernel, out_shape=jax.ShapeDtypeStruct((1, 8, 2048), F32),...  45.8 us
    unnamed x1, local copies, waits for them, and re-layouts  1.47 us

profile of v1, /device:TPU:1, one launch (start us, length us, event | category | flops | bytes accessed | tf_op | source)
XLA Modules:
  0.0 47.2 jit_solution(3195605528650221073)
XLA Ops:
  0.0 45.8 %ladder.1 = f32[1,8,2048]{2,1,0:T(8,128)} custom-call(bf16[8,64,4096]{2,1,0:T(8,128)(2,1)} %amp.1, bf16[4096,1024]{1,0:T(8,128)(2,1)} %vint.1, s32[64]{0:T(128)} %occ_ref.1, s32[32]{0:T(128)} %vir_ref.1), custom_call_target="tpu_custom_call" | custom-call | flops 5400000000 | bytes 13000000 | tf_op jit(solution)/shard_map/ladder/pallas_call | solution.py:239
  45.8 1.5 %copy.6 = f32[1,8,2048]{2,1,0:T(8,128)} copy(f32[1,8,2048]{2,1,0:T(8,128)} %ladder.1) | data formatting | bytes 131072

commit v2 on v1

--- a/solution.py
+++ b/solution.py
@@ -11,6 +11,7 @@
 F32, BF16, I32 = jnp.float32, jnp.bfloat16, jnp.int32
 CHIPS, Z, CORES, OCC = 16, 8, 2, 8
 NB = 32
+SLOTS = 12
 KC, NK = 512, 8
 
 
@@ -18,16 +19,30 @@
     return lax.broadcasted_iota(I32, shape, dim)
 
 
+def column(row, n):
+    return jnp.sum(jnp.where(iota((n, n), 0) == iota((n, n), 1), row, 0), axis=1, keepdims=True)
+
+
+def window(x, start, slots):
+    x = jnp.where((start & 16) != 0, jnp.concatenate([x[16:], x[:16]], axis=0), x)
+    x = jnp.where((start & 8) != 0, jnp.concatenate([x[8:], x[:8]], axis=0), x)[0:24]
+    x = jnp.where((start & 4) != 0, pltpu.roll(x, 20, 0), x)[0:16]
+    x = jnp.where((start & 2) != 0, pltpu.roll(x, 14, 0), x)
+    return jnp.where((start & 1) != 0, pltpu.roll(x, 15, 0), x)
+
+
 def kernel(
-    amp, vint, occ_ref, vir_ref, out_ref,
+    slots, amp, vint, occ_ref, vir_ref, out_ref,
     a_sib, a_own, v_buf, x_sib, x_own, x_got, hi, lo, sel, y_buf, y_got, u_buf, ut_buf,
-    m_buf, t_buf, m_got, t_got, flags,
+    m_buf, t_buf, m_got, t_got, flags, starts,
     sem_as, sem_ao, sem_v, s1_send, s1_recv, s2_send, s2_recv, s3_send, s3_recv, m_send, m_recv,
 ):
     occ = lax.axis_index("occ")
     vir = lax.axis_index("vir")
     chip = vir // CORES
     core = vir % CORES
+    dense = slots == NB
+    width = NB if dense else 16
     sibling = (occ, chip * CORES + 1 - core)
 
     def load_as(k):
@@ -54,12 +69,37 @@
                 to = ((occ + d) % OCC, chip * CORES + (core + c) % CORES)
                 pl.semaphore_signal(barrier, inc=1, device_id=to, device_id_type=MESH)
 
+    vir_row = vir_ref[...].reshape(1, NB)
+    occ_row = occ_ref[...].reshape(1, 64)
+    vir_col = column(vir_row, NB)
+    order = iota((NB, 1), 0)
+    rank_row = None
+    if not dense:
+        before = jnp.logical_or(vir_col < vir_row, jnp.logical_and(vir_col == vir_row, iota((NB, NB), 0) < iota((NB, NB), 1)))
+        place_row = jnp.sum(before.astype(F32), axis=0, keepdims=True)
+        same = jnp.logical_and(before, vir_col == vir_row)
+        rank_row = jnp.sum(same.astype(F32), axis=0, keepdims=True)
+        hit = iota((NB, NB), 0).astype(F32) == place_row
+        order = jnp.sum(jnp.where(hit, iota((NB, NB), 1).astype(F32), 0.0), axis=1, keepdims=True).astype(I32)
+        cols = iota((64, 256), 1)
+        at = iota((64, 256), 0)
+        occ_all = jnp.broadcast_to(occ_row.astype(F32), (8, 64))
+        row_i = jnp.dot(occ_all, (at == 8 * occ + cols // 32).astype(F32), preferred_element_type=F32)
+        row_j = jnp.dot(occ_all, (at == 32 * core + cols % 32).astype(F32), preferred_element_type=F32)
+        group = row_i.astype(I32) ^ row_j.astype(I32)
+        below = jnp.sum((vir_col < iota((NB, 8), 1)).astype(F32), axis=0, keepdims=True)
+        label = group[0:1, :] ^ vir_col
+        first_slot = jnp.zeros((NB, 256), F32)
+        for irrep in range(8):
+            first_slot = jnp.where(label == irrep, below[:, irrep:irrep + 1], first_slot)
+        starts[...] = first_slot.astype(I32)
+
     xh, zh = chip // Z, (chip % Z) // 4
     blocks = []
     for step, (dx, dz) in enumerate(((1, 1), (0, 1), (1, 0), (0, 0))):
         blocks.append(((xh + dx) % 2) * 2 + (zh + dz) % 2)
-    col, row = iota((NB, 1024), 1), iota((NB, 1024), 0)
-    direct, swapped = col - row, col - NB * row
+    col = iota((NB, 1024), 1)
+    direct, swapped = col - order, col - NB * order
     for step in range(4):
         def build(al, carry, step=step):
             a = blocks[step] * 8 + al
@@ -118,16 +158,25 @@
     for step in range(4):
         y = lax.dot_general(sel[step], hi[...], nt, preferred_element_type=F32)
         y = y + lax.dot_general(sel[step], lo[...], nt, preferred_element_type=F32)
-        y_buf[step] = y.reshape(4, 64, 256)
         for g in range(4):
+            parts = []
+            for n in range(2):
+                part = y[(2 * g + n) * NB:(2 * g + n + 1) * NB, :]
+                if not dense:
+                    part = window(part, starts[pl.ds(blocks[step] * 8 + 2 * g + n, 1), :], slots)
+                parts.append(part)
+            if dense:
+                y_buf[step, g, 0:NB, :], y_buf[step, g, NB:2 * NB, :] = parts
+            else:
+                y_buf[step, g, 0:8, :], y_buf[step, g, 8:16, :] = parts[0][0:8], parts[1][0:8]
+                if slots > 8:
+                    y_buf[step, g, 16:24, :] = jnp.where(
+                        iota((8, 256), 0) < 4, parts[0][8:16], pltpu.roll(parts[1][8:16], 4, 0))
             target, copy = s2_copy(step, g)
             if step < 3:
                 copy.start()
             else:
                 pl.when(target != chip)(copy.start)
-
-    occ_row = occ_ref[...].reshape(1, 64)
-    vir_row = vir_ref[...].reshape(1, NB)
 
     total = y_buf[3, chip % 4]
     for d in range(1, CHIPS):
@@ -137,24 +186,32 @@
             device_id=sibling, device_id_type=MESH)
         s2_in.wait_recv()
         total = total + y_got[d]
-    u_buf[0:64, :] = total
-    u_buf[64:128, :] = jnp.zeros((64, 256), F32)
+    u_buf[...] = jnp.zeros((128, 256), F32)
+    if dense:
+        u_buf[0:64, :] = total
+    else:
+        u_buf[0:8, :], u_buf[16:24, :] = total[0:8], total[8:16]
+        if slots > 8:
+            low = iota((8, 256), 0) < 4
+            u_buf[8:16, :] = jnp.where(low, total[16:24], 0.0)
+            u_buf[24:32, :] = jnp.where(low, pltpu.roll(total[16:24], 4, 0), 0.0)
     ut_buf[...] = jnp.transpose(u_buf[...])
 
-    lane = iota((8, 128), 1) // NB
+    lane = iota((8, 128), 1) // width
+    per = 128 // width
 
     def place(pieces, a):
         got = None
         for n, piece in enumerate(pieces):
-            shift = ((n - a) * NB) % 128
+            shift = ((n - a) * width) % 128
             moved = pltpu.roll(piece, shift, 1) if shift else piece
             got = moved if got is None else jnp.where(lane == n, moved, got)
         return got
 
     for jl in range(4):
-        for half in range(2):
+        for half in range(8 // per):
             lanes = pl.ds(half * 128, 128)
-            rows = [ut_buf[pl.ds((4 * half + n) * 32 + jl * 8, 8), :] for n in range(4)]
+            rows = [ut_buf[pl.ds((per * half + n) * 32 + jl * 8, 8), :] for n in range(per)]
             for a in range(2):
                 t_buf[a, jl, :, lanes] = place(rows, a)
 
@@ -175,9 +232,9 @@
             pl.when(here)(s3_local(jl, a).start)
 
     for jl in range(4):
-        for half in range(2):
+        for half in range(8 // per):
             lanes = pl.ds(half * 128, 128)
-            rows = [ut_buf[pl.ds(jl * 8 + half * 4 + n, 8, stride=32), :] for n in range(4)]
+            rows = [ut_buf[pl.ds(jl * 8 + half * per + n, 8, stride=32), :] for n in range(per)]
             for a in range(2):
                 m_buf[a, jl, :, lanes] = place(rows, a)
     m_copy = pltpu.make_async_remote_copy(
@@ -214,10 +271,19 @@
             pl.when(own)(s3_local(jl, a).wait)
     m_copy.wait_recv()
 
+    if not dense:
+        wide = jnp.broadcast_to(rank_row, (8, NB)).astype(F32)
+        ranks = jnp.dot(wide, (iota((NB, 256), 1) % NB == iota((NB, 256), 0)).astype(F32), preferred_element_type=F32)[0:1, :]
+        at, to = iota((128, 256), 0), iota((128, 256), 1)
+        spread = jnp.where(at // 16 == to // NB, ((at % 16).astype(F32) == ranks).astype(F32), 0.0).astype(BF16)
     for jl in range(4):
         for part, src in ((core, m_buf.at[core, jl]), (1 - core, m_got.at[jl])):
             j = part * 4 + jl
             value = src[...] - t_got[j]
+            if not dense:
+                top = value.astype(BF16)
+                rest = (value - top.astype(F32)).astype(BF16)
+                value = jnp.dot(top, spread, preferred_element_type=F32) + jnp.dot(rest, spread, preferred_element_type=F32)
             flag = flags[pl.ds(pl.multiple_of(j * 8, 8), 8), :]
             out_ref[0, :, pl.ds(pl.multiple_of(j * 256, 256), 256)] = jnp.where(flag > 0.5, value, 0.0)
 
@@ -232,12 +298,14 @@
                 pl.when(target != chip)(copy.wait_send)
 
 
-def shards(amplitudes, integrals, occ_irrep, vir_irrep):
+def ladder(slots, amplitudes, integrals, occ_irrep, vir_irrep):
     any_space = pl.BlockSpec(memory_space=pl.ANY)
     vmem = pl.BlockSpec(memory_space=pltpu.VMEM)
     dma = pltpu.SemaphoreType.DMA
+    rows = 2 * slots
+    lanes = 256 if slots == NB else 128
     return pl.pallas_call(
-        kernel,
+        functools.partial(kernel, slots),
         out_shape=jax.ShapeDtypeStruct((1, 8, 2048), F32),
         in_specs=[any_space, any_space, vmem, vmem],
         out_specs=vmem,
@@ -251,24 +319,33 @@
             pltpu.VMEM((256, 1024), BF16),
             pltpu.VMEM((256, 1024), BF16),
             pltpu.VMEM((4, 256, 1024), BF16),
-            pltpu.VMEM((4, 4, 64, 256), F32),
-            pltpu.VMEM((CHIPS, 64, 256), F32),
+            pltpu.VMEM((4, 4, rows, 256), F32),
+            pltpu.VMEM((CHIPS, rows, 256), F32),
             pltpu.VMEM((128, 256), F32),
             pltpu.VMEM((256, 128), F32),
-            pltpu.VMEM((2, 4, 8, 256), F32),
-            pltpu.VMEM((2, 4, 8, 256), F32),
-            pltpu.VMEM((4, 8, 256), F32),
-            pltpu.VMEM((8, 8, 256), F32),
+            pltpu.VMEM((2, 4, 8, lanes), F32),
+            pltpu.VMEM((2, 4, 8, lanes), F32),
+            pltpu.VMEM((4, 8, lanes), F32),
+            pltpu.VMEM((8, 8, lanes), F32),
             pltpu.VMEM((64, 256), F32),
+            pltpu.VMEM((NB, 256), I32),
             dma((NK,)), dma((1,)), dma((NK,)), dma, dma,
             dma((16,)), dma((16,)), dma((8,)), dma((8,)), dma, dma,
         ],
         compiler_params=pltpu.CompilerParams(
-            collective_id=0, has_side_effects=True, vmem_limit_bytes=56 << 20),
+            collective_id=slots, has_side_effects=True, vmem_limit_bytes=56 << 20),
         cost_estimate=pl.CostEstimate(
             flops=5_400_000_000, bytes_accessed=13_000_000, transcendentals=0),
-        name="ladder",
+        name="ladder%d" % slots,
     )(amplitudes, integrals, occ_irrep, vir_irrep)
+
+
+def shards(amplitudes, integrals, occ_irrep, vir_irrep):
+    same = vir_irrep[:, None] == vir_irrep[None, :]
+    most = jnp.max(jnp.sum(same.astype(I32), axis=1))
+    return lax.cond(
+        most <= SLOTS, functools.partial(ladder, SLOTS), functools.partial(ladder, NB),
+        amplitudes, integrals, occ_irrep, vir_irrep)
 
 
 def solution(mesh):

time: 47.4 us -> 35.3 us (0.74)
  Pallas kernels: 45.8 us -> 32.3 us
  other arithmetic: 0 us -> 1.55 us
  local copies, waits for them, and re-layouts: 1.47 us -> 0.63 us
  between operations: 0.01 us -> 0.66 us
    pallas_call x1, Pallas kernels: 45.8 us -> 32.3 us  [ladder(): pl.pallas_call(functools.partial(kernel, slots), out_shape=jax.ShapeDtype...]
    reduce_sum x0 -> x1, other arithmetic: none -> 0.91 us  [shards(): most = jnp.max(jnp.sum(same.astype(I32), axis=1))]
    unnamed x1, local copies, waits for them, and re-layouts: 1.47 us -> 0.63 us
    reduce_max x0 -> x1, other arithmetic: none -> 0.64 us  [shards(): most = jnp.max(jnp.sum(same.astype(I32), axis=1))]
where the time goes in v2:
time: 35.3 us; the launch traced here: 35.2 us
  Pallas kernels  32.3 us (92%)
  other arithmetic  1.55 us (4%)
  between operations  0.66 us (2%)
  local copies, waits for them, and re-layouts  0.63 us (2%)
    pallas_call x1, Pallas kernels, ladder(): pl.pallas_call(functools.partial(kernel, slots), out_shape=jax.ShapeDtype...  32.3 us
    reduce_sum x1, other arithmetic, shards(): most = jnp.max(jnp.sum(same.astype(I32), axis=1))  0.91 us

profile of v2, /device:TPU:1, one launch (start us, length us, event | category | flops | bytes accessed | tf_op | source)
XLA Modules:
  0.0 35.2 jit_solution(17938233554587974092)
XLA Ops:
  0.0 0.9 %convert_reduce_fusion = s32[32]{0:T(128)S(1)} fusion(s32[32]{0:T(128)} %param.9), kind=kLoop, calls=%fused_computation | loop fusion | flops 3040 | bytes 256 | tf_op jit(solution)/shard_map/reduce_sum | solution.py:345
  0.9 0.6 %reduce_max.9 = s32[]{:T(128)} reduce(s32[32]{0:T(128)S(1)} %convert_reduce_fusion, s32[]{:T(128)} %constant.1.clone.1), dimensions={0}, to_apply=%region_1.0 | reduce | flops 31 | bytes 136 | tf_op jit(solution)/shard_map/reduce_max | solution.py:345
  2.2 32.4 %conditional.1 = (f32[1,8,2048]{2,1,0:T(8,128)S(1)}) conditional(s32[]{:T(128)} %convert_element_type.7, (bf16[8,64,4096]{2,1,0:T(8,128)(2,1)}, bf16[4096,1024]{1,0:T(8,128)(2,1)}, s32[64]{0:T(128)}, s32[32]{0:T(128)}) %tuple.11, (bf16[8,64,4096]{2,1,0:T(8,128)(2,1)}, bf16[4096,1024]{1,0:T(8,128)(2,1)}, s32[64]{0:T(128)}, s32[32]{0:T(128)}) %tuple.11), branch_computations={%region_2.0_spmd, %region_3.0_spmd} | conditional | flops 5400000000 | bytes 13000008 | solution.py:346
  2.2 32.3 %ladder12.1 = f32[1,8,2048]{2,1,0:T(8,128)S(1)} custom-call(bf16[8,64,4096]{2,1,0:T(8,128)(2,1)} %get-tuple-element.28.amp, bf16[4096,1024]{1,0:T(8,128)(2,1)} %get-tuple-element.29.vint, s32[64]{0:T(128)} %get-tuple-element.30.occ_ref, s32[32]{0:T(128)} %get-tuple-element.31.vir_ref), custom_call_target="tpu_custom_call" | custom-call | flops 5400000000 | bytes 13000000 | tf_op jit(solution)/shard_map/cond/branch_1_fun/ladder12/pallas_call | solution.py:307
  34.6 0.6 %copy.10 = f32[1,8,2048]{2,1,0:T(8,128)} copy(f32[1,8,2048]{2,1,0:T(8,128)S(1)} %get-tuple-element.32) | data formatting | bytes 131072

commit v3 on v2

--- a/solution.py
+++ b/solution.py
@@ -11,8 +11,9 @@
 F32, BF16, I32 = jnp.float32, jnp.bfloat16, jnp.int32
 CHIPS, Z, CORES, OCC = 16, 8, 2, 8
 NB = 32
-SLOTS = 12
-KC, NK = 512, 8
+SLOTS = (8, 12)
+DEPTH = 4096
+CHUNKS = ((0, 512), (512, 1024), (1536, 1024), (2560, 1024), (3584, 512))
 
 
 def iota(shape, dim):
@@ -34,7 +35,7 @@
 def kernel(
     slots, amp, vint, occ_ref, vir_ref, out_ref,
     a_sib, a_own, v_buf, x_sib, x_own, x_got, hi, lo, sel, y_buf, y_got, u_buf, ut_buf,
-    m_buf, t_buf, m_got, t_got, flags, starts,
+    m_buf, t_buf, w_buf, t_got, flags, starts, spread,
     sem_as, sem_ao, sem_v, s1_send, s1_recv, s2_send, s2_recv, s3_send, s3_recv, m_send, m_recv,
 ):
     occ = lax.axis_index("occ")
@@ -46,15 +47,16 @@
     sibling = (occ, chip * CORES + 1 - core)
 
     def load_as(k):
+        part = pl.ds(*CHUNKS[k])
         return pltpu.make_async_copy(
-            amp.at[:, pl.ds(32 * (1 - core), 32), pl.ds(k * KC, KC)], a_sib.at[k], sem_as.at[k])
+            amp.at[:, pl.ds(32 * (1 - core), 32), part], a_sib.at[:, :, part], sem_as.at[k])
 
     def load_v(k):
-        return pltpu.make_async_copy(
-            vint.at[pl.ds(k * KC, KC), :], v_buf.at[pl.ds(k * KC, KC), :], sem_v.at[k])
+        part = pl.ds(*CHUNKS[k])
+        return pltpu.make_async_copy(vint.at[part, :], v_buf.at[part, :], sem_v.at[k])
 
     load_ao = pltpu.make_async_copy(amp.at[:, pl.ds(32 * core, 32), :], a_own, sem_ao.at[0])
-    for k in range(NK):
+    for k in range(len(CHUNKS)):
         load_as(k).start()
         load_v(k).start()
     load_ao.start()
@@ -109,23 +111,13 @@
             return carry
         lax.fori_loop(0, 8, build, 0)
 
-    def first(k, carry):
+    for k, (at, depth) in enumerate(CHUNKS):
         load_as(k).wait()
         load_v(k).wait()
-        lhs = a_sib[k].reshape(256, KC)
-        rhs = v_buf[pl.ds(pl.multiple_of(k * KC, KC), KC), :]
-        part = jnp.dot(lhs, rhs, preferred_element_type=F32)
-
-        @pl.when(k == 0)
-        def _():
-            x_sib[...] = part
-
-        @pl.when(k > 0)
-        def _():
-            x_sib[...] += part
-        return carry
-
-    lax.fori_loop(0, NK, first, 0)
+        part = jnp.dot(
+            a_sib[:, :, at:at + depth].reshape(256, depth), v_buf[at:at + depth, :],
+            preferred_element_type=F32)
+        x_sib[...] = part if k == 0 else x_sib[...] + part
     pl.semaphore_wait(barrier, CHIPS - 1 + OCC * CORES - 1)
     s1 = pltpu.make_async_remote_copy(
         src_ref=x_sib, dst_ref=x_got, send_sem=s1_send, recv_sem=s1_recv,
@@ -136,7 +128,7 @@
     for n in range(4):
         cols = pl.ds(n * 256, 256)
         x_own[:, cols] = jnp.dot(
-            a_own[...].reshape(256, NK * KC), v_buf[:, cols], preferred_element_type=F32)
+            a_own[...].reshape(256, DEPTH), v_buf[:, cols], preferred_element_type=F32)
     s1.wait_recv()
     for n in range(4):
         cols = pl.ds(n * 256, 256)
@@ -178,6 +170,26 @@
             else:
                 pl.when(target != chip)(copy.start)
 
+    to_j = (iota((64, 2048), 1) // NB == iota((64, 2048), 0)).astype(F32)
+    occ_all = jnp.broadcast_to(occ_row.astype(F32), (8, 64))
+    occ_j = jnp.dot(occ_all, to_j, preferred_element_type=F32)
+    to_b = (iota((NB, 2048), 1) % NB == iota((NB, 2048), 0)).astype(F32)
+    vir_all = jnp.broadcast_to(vir_row.astype(F32), (8, NB))
+    vir_b = jnp.dot(vir_all, to_b, preferred_element_type=F32)
+    mine = iota((8, 64), 1) == occ * 8 + iota((8, 64), 0)
+    occ_i = jnp.sum(jnp.where(mine, occ_all, 0.0), axis=1, keepdims=True)
+    vir_a = jnp.sum(jnp.where(iota((8, NB), 1) == vir, vir_all, 0.0), axis=1, keepdims=True)
+    left = occ_j.astype(I32) ^ vir_b.astype(I32)
+    right = occ_i.astype(I32) ^ vir_a.astype(I32)
+    keep = (left ^ right) == 0
+    for j in range(8):
+        flags[j * 8:j * 8 + 8, :] = jnp.where(keep[:, j * 256:(j + 1) * 256], 1.0, 0.0)
+
+    if not dense:
+        wide = jnp.broadcast_to(rank_row, (8, NB)).astype(F32)
+        ranks = jnp.dot(wide, (iota((NB, 256), 1) % NB == iota((NB, 256), 0)).astype(F32), preferred_element_type=F32)[0:1, :]
+        at, to = iota((128, 256), 0), iota((128, 256), 1)
+        spread[...] = jnp.where(at // 16 == to // NB, ((at % 16).astype(F32) == ranks).astype(F32), 0.0).astype(BF16)
     total = y_buf[3, chip % 4]
     for d in range(1, CHIPS):
         s2_in = pltpu.make_async_remote_copy(
@@ -208,85 +220,62 @@
             got = moved if got is None else jnp.where(lane == n, moved, got)
         return got
 
+    def s3_copy(jl, a):
+        return pltpu.make_async_remote_copy(
+            src_ref=t_buf.at[a, jl], dst_ref=t_got.at[occ],
+            send_sem=s3_send.at[a * 4 + jl], recv_sem=s3_recv.at[occ],
+            device_id=(4 * core + jl, chip * CORES + a), device_id_type=MESH)
+
+    def s3_here(jl, a):
+        return jnp.logical_and(4 * core + jl == occ, core == a)
+
     for jl in range(4):
         for half in range(8 // per):
             lanes = pl.ds(half * 128, 128)
             rows = [ut_buf[pl.ds((per * half + n) * 32 + jl * 8, 8), :] for n in range(per)]
             for a in range(2):
                 t_buf[a, jl, :, lanes] = place(rows, a)
-
-    def s3_copy(jl, a):
-        to = 4 * core + jl
-        return pltpu.make_async_remote_copy(
-            src_ref=t_buf.at[a, jl], dst_ref=t_got.at[occ],
-            send_sem=s3_send.at[a * 4 + jl], recv_sem=s3_recv.at[occ],
-            device_id=(to, chip * CORES + a), device_id_type=MESH)
-
-    def s3_local(jl, a):
-        return pltpu.make_async_copy(t_buf.at[a, jl], t_got.at[occ], s3_send.at[a * 4 + jl])
-
-    for jl in range(4):
         for a in range(2):
-            here = jnp.logical_and(4 * core + jl == occ, core == a)
-            pl.when(jnp.logical_not(here))(s3_copy(jl, a).start)
-            pl.when(here)(s3_local(jl, a).start)
+            pl.when(jnp.logical_not(s3_here(jl, a)))(s3_copy(jl, a).start)
 
     for jl in range(4):
         for half in range(8 // per):
             lanes = pl.ds(half * 128, 128)
             rows = [ut_buf[pl.ds(jl * 8 + half * per + n, 8, stride=32), :] for n in range(per)]
-            for a in range(2):
-                m_buf[a, jl, :, lanes] = place(rows, a)
+            zero, one = place(rows, 0), place(rows, 1)
+            m_buf[jl, :, lanes] = jnp.where(core == 0, one, zero)
+            w_buf[4 * core + jl, :, lanes] = jnp.where(core == 0, zero, one)
     m_copy = pltpu.make_async_remote_copy(
-        src_ref=m_buf.at[1 - core], dst_ref=m_got, send_sem=m_send, recv_sem=m_recv,
+        src_ref=m_buf, dst_ref=w_buf.at[pl.ds(4 * core, 4)], send_sem=m_send, recv_sem=m_recv,
         device_id=sibling, device_id_type=MESH)
     m_copy.start()
-
-    spread = (iota((64, 2048), 1) // NB == iota((64, 2048), 0)).astype(F32)
-    occ_all = jnp.broadcast_to(occ_row.astype(F32), (8, 64))
-    occ_j = jnp.dot(occ_all, spread, preferred_element_type=F32)
-    spread = (iota((NB, 2048), 1) % NB == iota((NB, 2048), 0)).astype(F32)
-    vir_all = jnp.broadcast_to(vir_row.astype(F32), (8, NB))
-    vir_b = jnp.dot(vir_all, spread, preferred_element_type=F32)
-    mine = iota((8, 64), 1) == occ * 8 + iota((8, 64), 0)
-    occ_i = jnp.sum(jnp.where(mine, occ_all, 0.0), axis=1, keepdims=True)
-    vir_a = jnp.sum(jnp.where(iota((8, NB), 1) == vir, vir_all, 0.0), axis=1, keepdims=True)
-    left = occ_j.astype(I32) ^ vir_b.astype(I32)
-    right = occ_i.astype(I32) ^ vir_a.astype(I32)
-    keep = (left ^ right) == 0
-    for j in range(8):
-        flags[j * 8:j * 8 + 8, :] = jnp.where(keep[:, j * 256:(j + 1) * 256], 1.0, 0.0)
-
-    here = (occ // 4 == core)
+    for jl in range(4):
+        for a in range(2):
+            @pl.when(s3_here(jl, a))
+            def _(jl=jl, a=a):
+                t_got[occ] = t_buf[a, jl]
+
+    m_copy.wait_recv()
     for d in range(OCC):
         incoming = pltpu.make_async_remote_copy(
             src_ref=t_buf.at[0, 0], dst_ref=t_got.at[d], send_sem=s3_send.at[0],
             recv_sem=s3_recv.at[d], device_id=sibling, device_id_type=MESH)
-        local = jnp.logical_and(here, occ == d)
+        local = jnp.logical_and(occ // 4 == core, occ == d)
         pl.when(jnp.logical_not(local))(incoming.wait_recv)
+
+    value = (w_buf[...] - t_got[...]).reshape(64, 8 * width)
+    if not dense:
+        top = value.astype(BF16)
+        rest = (value - top.astype(F32)).astype(BF16)
+        value = jnp.dot(jnp.concatenate([top, rest], axis=0), spread[...], preferred_element_type=F32)
+        value = value[:64] + value[64:]
+    value = jnp.where(flags[...] > 0.5, value, 0.0)
+    for j in range(OCC):
+        out_ref[0, :, j * 256:(j + 1) * 256] = value[j * 8:(j + 1) * 8]
+
     for jl in range(4):
         for a in range(2):
-            own = jnp.logical_and(4 * core + jl == occ, core == a)
-            pl.when(jnp.logical_not(own))(s3_copy(jl, a).wait_send)
-            pl.when(own)(s3_local(jl, a).wait)
-    m_copy.wait_recv()
-
-    if not dense:
-        wide = jnp.broadcast_to(rank_row, (8, NB)).astype(F32)
-        ranks = jnp.dot(wide, (iota((NB, 256), 1) % NB == iota((NB, 256), 0)).astype(F32), preferred_element_type=F32)[0:1, :]
-        at, to = iota((128, 256), 0), iota((128, 256), 1)
-        spread = jnp.where(at // 16 == to // NB, ((at % 16).astype(F32) == ranks).astype(F32), 0.0).astype(BF16)
-    for jl in range(4):
-        for part, src in ((core, m_buf.at[core, jl]), (1 - core, m_got.at[jl])):
-            j = part * 4 + jl
-            value = src[...] - t_got[j]
-            if not dense:
-                top = value.astype(BF16)
-                rest = (value - top.astype(F32)).astype(BF16)
-                value = jnp.dot(top, spread, preferred_element_type=F32) + jnp.dot(rest, spread, preferred_element_type=F32)
-            flag = flags[pl.ds(pl.multiple_of(j * 8, 8), 8), :]
-            out_ref[0, :, pl.ds(pl.multiple_of(j * 256, 256), 256)] = jnp.where(flag > 0.5, value, 0.0)
-
+            pl.when(jnp.logical_not(s3_here(jl, a)))(s3_copy(jl, a).wait_send)
     m_copy.wait_send()
     s1.wait_send()
     for step in range(4):
@@ -310,9 +299,9 @@
         in_specs=[any_space, any_space, vmem, vmem],
         out_specs=vmem,
         scratch_shapes=[
-            pltpu.VMEM((NK, 8, 32, KC), BF16),
-            pltpu.VMEM((8, 32, NK * KC), BF16),
-            pltpu.VMEM((NK * KC, 1024), BF16),
+            pltpu.VMEM((8, 32, DEPTH), BF16),
+            pltpu.VMEM((8, 32, DEPTH), BF16),
+            pltpu.VMEM((DEPTH, 1024), BF16),
             pltpu.VMEM((256, 1024), F32),
             pltpu.VMEM((256, 1024), F32),
             pltpu.VMEM((256, 1024), F32),
@@ -323,13 +312,14 @@
             pltpu.VMEM((CHIPS, rows, 256), F32),
             pltpu.VMEM((128, 256), F32),
             pltpu.VMEM((256, 128), F32),
+            pltpu.VMEM((4, 8, lanes), F32),
             pltpu.VMEM((2, 4, 8, lanes), F32),
-            pltpu.VMEM((2, 4, 8, lanes), F32),
-            pltpu.VMEM((4, 8, lanes), F32),
+            pltpu.VMEM((8, 8, lanes), F32),
             pltpu.VMEM((8, 8, lanes), F32),
             pltpu.VMEM((64, 256), F32),
             pltpu.VMEM((NB, 256), I32),
-            dma((NK,)), dma((1,)), dma((NK,)), dma, dma,
+            pltpu.VMEM((128, 256), BF16),
+            dma((len(CHUNKS),)), dma((1,)), dma((len(CHUNKS),)), dma, dma,
             dma((16,)), dma((16,)), dma((8,)), dma((8,)), dma, dma,
         ],
         compiler_params=pltpu.CompilerParams(
@@ -341,11 +331,10 @@
 
 
 def shards(amplitudes, integrals, occ_irrep, vir_irrep):
-    same = vir_irrep[:, None] == vir_irrep[None, :]
-    most = jnp.max(jnp.sum(same.astype(I32), axis=1))
-    return lax.cond(
-        most <= SLOTS, functools.partial(ladder, SLOTS), functools.partial(ladder, NB),
-        amplitudes, integrals, occ_irrep, vir_irrep)
+    most = jnp.max(jnp.sum((vir_irrep[:, None] == vir_irrep[None, :]).astype(I32), axis=1))
+    args = (amplitudes, integrals, occ_irrep, vir_irrep)
+    wide = functools.partial(lax.cond, most <= SLOTS[1], functools.partial(ladder, SLOTS[1]), functools.partial(ladder, NB))
+    return lax.cond(most <= SLOTS[0], functools.partial(ladder, SLOTS[0]), wide, *args)
 
 
 def solution(mesh):

time: 35.3 us -> 32.3 us (0.915)
  Pallas kernels: 32.3 us -> 28.9 us
  loops' own time: 0.02 us -> 0.42 us
    pallas_call x1, Pallas kernels: 32.3 us -> 28.9 us  [ladder(): pl.pallas_call(functools.partial(kernel, slots), out_shape=jax.ShapeDtype...]
    another operation x1, loops' own time: 0.02 us -> 0.42 us  [shards(): lax.cond(most <= SLOTS[0], functools.partial(ladder, SLOTS[0]), wide, *args)]
where the time goes in v3:
time: 32.3 us; the launch traced here: 32.2 us
  Pallas kernels  28.9 us (89%)
  other arithmetic  1.55 us (5%)
  between operations  0.66 us (2%)
  local copies, waits for them, and re-layouts  0.63 us (2%)
  loops' own time  0.42 us (1%)
    pallas_call x1, Pallas kernels, ladder(): pl.pallas_call(functools.partial(kernel, slots), out_shape=jax.ShapeDtype...  28.9 us
    reduce_sum x1, other arithmetic, shards(): jnp.sum((vir_irrep[:, None] == vir_irrep[None, :]).astype(I32), axis=1)  0.91 us

profile of v3, /device:TPU:1, one launch (start us, length us, event | category | flops | bytes accessed | tf_op | source)
XLA Modules:
  0.0 32.2 jit_solution(8220163447500532068)
XLA Ops:
  0.0 0.9 %convert_reduce_fusion = s32[32]{0:T(128)S(1)} fusion(s32[32]{0:T(128)} %param.11), kind=kLoop, calls=%fused_computation | loop fusion | flops 3040 | bytes 256 | tf_op jit(solution)/shard_map/reduce_sum | solution.py:334
  0.9 0.6 %reduce_max.9 = s32[]{:T(128)} reduce(s32[32]{0:T(128)S(1)} %convert_reduce_fusion, s32[]{:T(128)} %constant.8.clone.1), dimensions={0}, to_apply=%region_1.0 | reduce | flops 31 | bytes 136 | tf_op jit(solution)/shard_map/reduce_max | solution.py:334
  2.2 29.3 %conditional.2 = (f32[1,8,2048]{2,1,0:T(8,128)S(1)}) conditional(s32[]{:T(128)} %convert_element_type.11, (s32[]{:T(128)}, bf16[8,64,4096]{2,1,0:T(8,128)(2,1)}, bf16[4096,1024]{1,0:T(8,128)(2,1)}, s32[64]{0:T(128)}, s32[32]{0:T(128)}) %tuple.19, (bf16[8,64,4096]{2,1,0:T(8,128)(2,1)}, bf16[4096,1024]{1,0:T(8,128)(2,1)}, s32[64]{0:T(128)}, ...), branch_computations={%region_2.0_spmd, %region_5.0_spmd} | conditional | flops 5400000000 | bytes 13000054 | solution.py:337
  2.4 28.9 %ladder8.1 = f32[1,8,2048]{2,1,0:T(8,128)S(1)} custom-call(bf16[8,64,4096]{2,1,0:T(8,128)(2,1)} %get-tuple-element.70.amp, bf16[4096,1024]{1,0:T(8,128)(2,1)} %get-tuple-element.71.vint, s32[64]{0:T(128)} %get-tuple-element.72.occ_ref, s32[32]{0:T(128)} %get-tuple-element.73.vir_ref), custom_call_target="tpu_custom_call" | custom-call | flops 5400000000 | bytes 13000000 | tf_op jit(solution)/shard_map/cond/branch_1_fun/ladder8/pallas_call | solution.py:296
  31.5 0.6 %copy.12 = f32[1,8,2048]{2,1,0:T(8,128)} copy(f32[1,8,2048]{2,1,0:T(8,128)S(1)} %get-tuple-element.74) | data formatting | bytes 131072

commit v4 on v3

--- a/solution.py
+++ b/solution.py
@@ -14,6 +14,11 @@
 SLOTS = (8, 12)
 DEPTH = 4096
 CHUNKS = ((0, 512), (512, 1024), (1536, 1024), (2560, 1024), (3584, 512))
+EARLY, LATE = (0,), (1, 2, 3, 4)
+NB = 32
+SLOTS = (8, 12)
+DEPTH = 4096
+CHUNKS = ((0, 512), (512, 1024), (1536, 1024), (2560, 1024), (3584, 512))
 
 
 def iota(shape, dim):
@@ -33,10 +38,10 @@
 
 
 def kernel(
-    slots, amp, vint, occ_ref, vir_ref, out_ref,
-    a_sib, a_own, v_buf, x_sib, x_own, x_got, hi, lo, sel, y_buf, y_got, u_buf, ut_buf,
+    slots, amp, vint, occ_in, vir_in, out_ref,
+    occ_ref, vir_ref,    a_sib, a_own, v_buf, x_sib, x_own, x_got, hi, lo, sel, y_buf, y_got, u_buf, ut_buf,
     m_buf, t_buf, w_buf, t_got, flags, starts, spread,
-    sem_as, sem_ao, sem_v, s1_send, s1_recv, s2_send, s2_recv, s3_send, s3_recv, m_send, m_recv,
+    sem_lab, sem_as, sem_ao, sem_v, s1_send, s1_recv, s2_send, s2_recv, s3_send, s3_recv, m_send, m_recv,
 ):
     occ = lax.axis_index("occ")
     vir = lax.axis_index("vir")
@@ -55,11 +60,23 @@
         part = pl.ds(*CHUNKS[k])
         return pltpu.make_async_copy(vint.at[part, :], v_buf.at[part, :], sem_v.at[k])
 
-    load_ao = pltpu.make_async_copy(amp.at[:, pl.ds(32 * core, 32), :], a_own, sem_ao.at[0])
+    def load_ao(k):
+        part = pl.ds(*CHUNKS[k])
+        return pltpu.make_async_copy(
+            amp.at[:, pl.ds(32 * core, 32), part], a_own.at[:, :, part], sem_ao.at[k])
+
+    labels = [pltpu.make_async_copy(src, dst, sem_lab.at[n])
+              for n, (src, dst) in enumerate(((occ_in, occ_ref), (vir_in, vir_ref)))]
     for k in range(len(CHUNKS)):
         load_as(k).start()
         load_v(k).start()
-    load_ao.start()
+        if k == 0:
+            for copy in labels:
+                copy.start()
+        if k in EARLY:
+            load_ao(k).start()
+    for k in LATE:
+        load_ao(k).start()
 
     barrier = pltpu.get_barrier_semaphore()
     for d in range(1, CHIPS):
@@ -71,6 +88,8 @@
                 to = ((occ + d) % OCC, chip * CORES + (core + c) % CORES)
                 pl.semaphore_signal(barrier, inc=1, device_id=to, device_id_type=MESH)
 
+    for copy in labels:
+        copy.wait()
     vir_row = vir_ref[...].reshape(1, NB)
     occ_row = occ_ref[...].reshape(1, 64)
     vir_col = column(vir_row, NB)
@@ -118,17 +137,25 @@
             a_sib[:, :, at:at + depth].reshape(256, depth), v_buf[at:at + depth, :],
             preferred_element_type=F32)
         x_sib[...] = part if k == 0 else x_sib[...] + part
+        if k in EARLY:
+            load_ao(k).wait()
+            part = jnp.dot(
+                a_own[:, :, at:at + depth].reshape(256, depth), v_buf[at:at + depth, :],
+                preferred_element_type=F32)
+            x_own[...] = part if k == 0 else x_own[...] + part
     pl.semaphore_wait(barrier, CHIPS - 1 + OCC * CORES - 1)
     s1 = pltpu.make_async_remote_copy(
         src_ref=x_sib, dst_ref=x_got, send_sem=s1_send, recv_sem=s1_recv,
         device_id=sibling, device_id_type=MESH)
     s1.start()
 
-    load_ao.wait()
+    for k in LATE:
+        load_ao(k).wait()
+    rest = CHUNKS[LATE[0]][0]
     for n in range(4):
         cols = pl.ds(n * 256, 256)
-        x_own[:, cols] = jnp.dot(
-            a_own[...].reshape(256, DEPTH), v_buf[:, cols], preferred_element_type=F32)
+        x_own[:, cols] += jnp.dot(
+            a_own[:, :, rest:].reshape(256, DEPTH - rest), v_buf[rest:, cols], preferred_element_type=F32)
     s1.wait_recv()
     for n in range(4):
         cols = pl.ds(n * 256, 256)
@@ -296,9 +323,11 @@
     return pl.pallas_call(
         functools.partial(kernel, slots),
         out_shape=jax.ShapeDtypeStruct((1, 8, 2048), F32),
-        in_specs=[any_space, any_space, vmem, vmem],
+        in_specs=[any_space] * 4,
         out_specs=vmem,
         scratch_shapes=[
+            pltpu.VMEM((64,), I32),
+            pltpu.VMEM((NB,), I32),
             pltpu.VMEM((8, 32, DEPTH), BF16),
             pltpu.VMEM((8, 32, DEPTH), BF16),
             pltpu.VMEM((DEPTH, 1024), BF16),
@@ -319,7 +348,7 @@
             pltpu.VMEM((64, 256), F32),
             pltpu.VMEM((NB, 256), I32),
             pltpu.VMEM((128, 256), BF16),
-            dma((len(CHUNKS),)), dma((1,)), dma((len(CHUNKS),)), dma, dma,
+            dma((2,)), dma((len(CHUNKS),)), dma((len(CHUNKS),)), dma((len(CHUNKS),)), dma, dma,
             dma((16,)), dma((16,)), dma((8,)), dma((8,)), dma, dma,
         ],
         compiler_params=pltpu.CompilerParams(

time: 32.3 us -> 31.4 us (0.972)
  Pallas kernels: 28.9 us -> 28.3 us
    pallas_call x1, Pallas kernels: 28.9 us -> 28.3 us  [ladder(): pl.pallas_call(functools.partial(kernel, slots), out_shape=jax.ShapeDtype...]
where the time goes in v4:
time: 31.4 us; the launch traced here: 31.3 us
  Pallas kernels  28.3 us (90%)
  other arithmetic  1.55 us (5%)
  between operations  0.66 us (2%)
  local copies, waits for them, and re-layouts  0.63 us (2%)
    pallas_call x1, Pallas kernels, ladder(): pl.pallas_call(functools.partial(kernel, slots), out_shape=jax.ShapeDtype...  28.3 us
    reduce_sum x1, other arithmetic, shards(): jnp.sum((vir_irrep[:, None] == vir_irrep[None, :]).astype(I32), axis=1)  0.91 us
    reduce_max x1, other arithmetic, shards(): jnp.max(jnp.sum((vir_irrep[:, None] == vir_irrep[None, :]).astype(I32), a...  0.64 us
    unnamed x1, local copies, waits for them, and re-layouts  0.63 us

profile of v4, /device:TPU:1, one launch (start us, length us, event | category | flops | bytes accessed | tf_op | source)
XLA Modules:
  0.0 31.3 jit_solution(254236397202110951)
XLA Ops:
  0.0 0.9 %convert_reduce_fusion = s32[32]{0:T(128)S(1)} fusion(s32[32]{0:T(128)} %param.11), kind=kLoop, calls=%fused_computation | loop fusion | flops 3040 | bytes 256 | tf_op jit(solution)/shard_map/reduce_sum | solution.py:363
  0.9 0.6 %reduce_max.9 = s32[]{:T(128)} reduce(s32[32]{0:T(128)S(1)} %convert_reduce_fusion, s32[]{:T(128)} %constant.8.clone.1), dimensions={0}, to_apply=%region_1.0 | reduce | flops 31 | bytes 136 | tf_op jit(solution)/shard_map/reduce_max | solution.py:363
  2.2 28.5 %conditional.2 = (f32[1,8,2048]{2,1,0:T(8,128)S(1)}) conditional(s32[]{:T(128)} %convert_element_type.11, (s32[]{:T(128)}, bf16[8,64,4096]{2,1,0:T(8,128)(2,1)}, bf16[4096,1024]{1,0:T(8,128)(2,1)}, s32[64]{0:T(128)}, s32[32]{0:T(128)}) %tuple.19, (bf16[8,64,4096]{2,1,0:T(8,128)(2,1)}, bf16[4096,1024]{1,0:T(8,128)(2,1)}, s32[64]{0:T(128)}, ...), branch_computations={%region_2.0_spmd, %region_5.0_spmd} | conditional | flops 5400000000 | bytes 13000054 | solution.py:366
  2.4 28.3 %ladder8.1 = f32[1,8,2048]{2,1,0:T(8,128)S(1)} custom-call(bf16[8,64,4096]{2,1,0:T(8,128)(2,1)} %get-tuple-element.70.amp, bf16[4096,1024]{1,0:T(8,128)(2,1)} %get-tuple-element.71.vint, s32[64]{0:T(128)} %get-tuple-element.72.occ_in, s32[32]{0:T(128)} %get-tuple-element.73.vir_in), custom_call_target="tpu_custom_call" | custom-call | flops 5400000000 | bytes 13000000 | tf_op jit(solution)/shard_map/cond/branch_1_fun/ladder8/pallas_call | solution.py:323
  30.7 0.6 %copy.12 = f32[1,8,2048]{2,1,0:T(8,128)} copy(f32[1,8,2048]{2,1,0:T(8,128)S(1)} %get-tuple-element.74) | data formatting | bytes 131072

commit v5 on v4

--- a/solution.py
+++ b/solution.py
@@ -312,6 +312,20 @@
                 copy.wait_send()
             else:
                 pl.when(target != chip)(copy.wait_send)
+
+
+def count(vir_ref, out_ref):
+    low = high = 0
+    for b in range(NB):
+        irrep = vir_ref[b]
+        one = jnp.left_shift(1, 6 * (irrep & 3))
+        low = low + jnp.where(irrep < 4, one, 0)
+        high = high + jnp.where(irrep < 4, 0, one)
+    most = 0
+    for n in range(4):
+        for word in (low, high):
+            most = jnp.maximum(most, (word >> (6 * n)) & 63)
+    out_ref[0] = most
 
 
 def ladder(slots, amplitudes, integrals, occ_irrep, vir_irrep):
@@ -360,9 +374,13 @@
 
 
 def shards(amplitudes, integrals, occ_irrep, vir_irrep):
-    most = jnp.max(jnp.sum((vir_irrep[:, None] == vir_irrep[None, :]).astype(I32), axis=1))
+    most = pl.pallas_call(
+        count, out_shape=jax.ShapeDtypeStruct((1,), I32),
+        in_specs=[pl.BlockSpec(memory_space=pltpu.SMEM)], out_specs=pl.BlockSpec(memory_space=pltpu.SMEM),
+        name="count")(vir_irrep)[0]
     args = (amplitudes, integrals, occ_irrep, vir_irrep)
-    wide = functools.partial(lax.cond, most <= SLOTS[1], functools.partial(ladder, SLOTS[1]), functools.partial(ladder, NB))
+    wide = functools.partial(
+        lax.cond, most <= SLOTS[1], functools.partial(ladder, SLOTS[1]), functools.partial(ladder, NB))
     return lax.cond(most <= SLOTS[0], functools.partial(ladder, SLOTS[0]), wide, *args)
 
 

time: 31.4 us -> 31.2 us (level)
  other arithmetic: 1.55 us -> 0 us
  Pallas kernels: 28.3 us -> 29.6 us
    pallas_call x0 -> x1, Pallas kernels: none -> 1.28 us  [shards(): pl.pallas_call(count, out_shape=jax.ShapeDtypeStruct((1,), I32), in_specs...]
    reduce_sum x1 -> x0, other arithmetic: 0.91 us -> none  [shards(): jnp.sum((vir_irrep[:, None] == vir_irrep[None, :]).astype(I32), axis=1)]
    reduce_max x1 -> x0, other arithmetic: 0.64 us -> none  [shards(): jnp.max(jnp.sum((vir_irrep[:, None] == vir_irrep[None, :]).astype(I32), a...]
where the time goes in v5:
time: 31.2 us; the launch traced here: 31.1 us
  Pallas kernels  29.6 us (95%)
  between operations  0.67 us (2%)
  local copies, waits for them, and re-layouts  0.63 us (2%)
    pallas_call x1, Pallas kernels, ladder(): pl.pallas_call(functools.partial(kernel, slots), out_shape=jax.ShapeDtype...  28.3 us
    pallas_call x1, Pallas kernels, shards(): pl.pallas_call(count, out_shape=jax.ShapeDtypeStruct((1,), I32), in_specs...  1.28 us
    unnamed x1, local copies, waits for them, and re-layouts  0.63 us

profile of v5, /device:TPU:1, one launch (start us, length us, event | category | flops | bytes accessed | tf_op | source)
XLA Modules:
  0.0 31.1 jit_solution(14574785955898628250)
XLA Ops:
  0.0 1.3 %count.1 = s32[1]{0:T(128)} custom-call(s32[32]{0:T(128)} %vir_ref.1), custom_call_target="tpu_custom_call" | custom-call | tf_op jit(solution)/shard_map/count/pallas_call | solution.py:377
  1.9 28.5 %conditional.2 = (f32[1,8,2048]{2,1,0:T(8,128)S(1)}) conditional(s32[]{:T(128)} %convert_element_type.7, (s32[]{:T(128)}, bf16[8,64,4096]{2,1,0:T(8,128)(2,1)}, bf16[4096,1024]{1,0:T(8,128)(2,1)}, s32[64]{0:T(128)}, s32[32]{0:T(128)}) %tuple.19, (bf16[8,64,4096]{2,1,0:T(8,128)(2,1)}, bf16[4096,1024]{1,0:T(8,128)(2,1)}, s32[64]{0:T(128)}, ...), branch_computations={%region_0.0_spmd, %region_3.0_spmd} | conditional | flops 5400000000 | bytes 13000054 | solution.py:384
  2.1 28.3 %ladder8.1 = f32[1,8,2048]{2,1,0:T(8,128)S(1)} custom-call(bf16[8,64,4096]{2,1,0:T(8,128)(2,1)} %get-tuple-element.70.amp, bf16[4096,1024]{1,0:T(8,128)(2,1)} %get-tuple-element.71.vint, s32[64]{0:T(128)} %get-tuple-element.72.occ_in, s32[32]{0:T(128)} %get-tuple-element.73.vir_in), custom_call_target="tpu_custom_call" | custom-call | flops 5400000000 | bytes 13000000 | tf_op jit(solution)/shard_map/cond/branch_1_fun/ladder8/pallas_call | solution.py:337
  30.4 0.6 %copy.12 = f32[1,8,2048]{2,1,0:T(8,128)} copy(f32[1,8,2048]{2,1,0:T(8,128)S(1)} %get-tuple-element.74) | data formatting | bytes 131072

commit v6 on v5

--- a/solution.py
+++ b/solution.py
@@ -117,7 +117,7 @@
 
     xh, zh = chip // Z, (chip % Z) // 4
     blocks = []
-    for step, (dx, dz) in enumerate(((1, 1), (0, 1), (1, 0), (0, 0))):
+    for step, (dx, dz) in enumerate(((1, 1), (1, 0), (0, 1), (0, 0))):
         blocks.append(((xh + dx) % 2) * 2 + (zh + dz) % 2)
     col = iota((NB, 1024), 1)
     direct, swapped = col - order, col - NB * order

time: 31.2 us -> 30.9 us (level)
  no operation moved by 1% of the time
where the time goes in v6:
time: 30.9 us; the launch traced here: 30.8 us
  Pallas kernels  29.3 us (95%)
  between operations  0.67 us (2%)
  local copies, waits for them, and re-layouts  0.63 us (2%)
    pallas_call x1, Pallas kernels, ladder(): pl.pallas_call(functools.partial(kernel, slots), out_shape=jax.ShapeDtype...  28 us
    pallas_call x1, Pallas kernels, shards(): pl.pallas_call(count, out_shape=jax.ShapeDtypeStruct((1,), I32), in_specs...  1.28 us
    unnamed x1, local copies, waits for them, and re-layouts  0.63 us

profile of v6, /device:TPU:1, one launch (start us, length us, event | category | flops | bytes accessed | tf_op | source)
XLA Modules:
  0.0 30.8 jit_solution(9833343283167540958)
XLA Ops:
  0.0 1.3 %count.1 = s32[1]{0:T(128)} custom-call(s32[32]{0:T(128)} %vir_ref.1), custom_call_target="tpu_custom_call" | custom-call | tf_op jit(solution)/shard_map/count/pallas_call | solution.py:377
  1.9 28.2 %conditional.2 = (f32[1,8,2048]{2,1,0:T(8,128)S(1)}) conditional(s32[]{:T(128)} %convert_element_type.7, (s32[]{:T(128)}, bf16[8,64,4096]{2,1,0:T(8,128)(2,1)}, bf16[4096,1024]{1,0:T(8,128)(2,1)}, s32[64]{0:T(128)}, s32[32]{0:T(128)}) %tuple.19, (bf16[8,64,4096]{2,1,0:T(8,128)(2,1)}, bf16[4096,1024]{1,0:T(8,128)(2,1)}, s32[64]{0:T(128)}, ...), branch_computations={%region_0.0_spmd, %region_3.0_spmd} | conditional | flops 5400000000 | bytes 13000054 | solution.py:384
  2.1 28.0 %ladder8.1 = f32[1,8,2048]{2,1,0:T(8,128)S(1)} custom-call(bf16[8,64,4096]{2,1,0:T(8,128)(2,1)} %get-tuple-element.70.amp, bf16[4096,1024]{1,0:T(8,128)(2,1)} %get-tuple-element.71.vint, s32[64]{0:T(128)} %get-tuple-element.72.occ_in, s32[32]{0:T(128)} %get-tuple-element.73.vir_in), custom_call_target="tpu_custom_call" | custom-call | flops 5400000000 | bytes 13000000 | tf_op jit(solution)/shard_map/cond/branch_1_fun/ladder8/pallas_call | solution.py:337
  30.2 0.6 %copy.12 = f32[1,8,2048]{2,1,0:T(8,128)} copy(f32[1,8,2048]{2,1,0:T(8,128)S(1)} %get-tuple-element.74) | data formatting | bytes 131072
